TPU v7x, 32 devices: a whole 2x2x4 slice. The times are simulated.
32 devices in a mesh: pb: 4 (over x, core), pa: 8 (over z, y).
Axes of the slice: x: 2, y: 2, z: 4, core: 2. Of those that a mesh axis runs over, the one named last changes fastest.
Arguments:
- passages: bfloat16 [16384, 768], P(('pb', 'pa')), may hold values from -6 to 6
- queries: bfloat16 [4096, 768], P(('pb', 'pa')), may hold values from -6 to 6
- passage_ids: int32 [16384], P(('pb', 'pa')), may hold values from 0 to 30521, as said below
- query_ids: int32 [4096], P(('pb', 'pa')), may hold values from 0 to 30521, as said below
- batch_length: int32 [16], replicated, may hold values from 128 to 512, as said below
- query_batch: int32 [128], P(('pb', 'pa')), may hold values from 0 to 3
- project_in: bfloat16 [768, 2304], replicated, may hold values from -0.21875 to 0.21875
- project_out: bfloat16 [768, 768], replicated, may hold values from -1.25 to 1.25
- expand_weight: bfloat16 [768, 3072], replicated, may hold values from -0.21875 to 0.21875
- expand_bias: float32 [3072], replicated, may hold values from -3 to 3
- reduce_weight: bfloat16 [3072, 768], replicated, may hold values from -0.109375 to 0.109375
- norm_gains: float32 [2, 768], replicated, may hold values from 0.5 to 1.5
- biases: float32 [6, 768], replicated, may hold values from -1.25 to 1.25
- term_weight: float32 [768], replicated, may hold values from -0.21875 to 0.21875
- term_bias: float32 [1], replicated, may hold values from -3 to 3
- out_grad: bfloat16 [16384, 768], P(('pb', 'pa')), may hold values from -6 to 6
- score_grad: float32 [128, 32], P('pb', 'pa'), may hold values from -6 to 6
Outputs:
- scores: float32 [128, 32], P('pb', 'pa')
- passage_out: bfloat16 [16384, 768], P(('pb', 'pa'))
- passage_grad: bfloat16 [16384, 768], P(('pb', 'pa'))
- query_grad: bfloat16 [4096, 768], P(('pb', 'pa'))
- project_in_grad: float32 [768, 2304], P('pa')
- project_out_grad: float32 [768, 768], P('pa')
- expand_grad: float32 [768, 3072], P('pa')
- expand_bias_grad: float32 [3072], P('pa')
- reduce_grad: float32 [3072, 768], P('pa')
- gains_grad: float32 [2, 768], P(None, 'pa')
- biases_grad: float32 [6, 768], P(None, 'pa')
- term_weight_grad: float32 [768], P('pa')
- term_bias_grad: float32 [1], replicated
Inputs may be any that keep to these rules, and one draw needn't show every extreme that they name: passage_ids and query_ids share which ids are frequent. `query_ids`: they share their frequent ids with passage_ids. `batch_length`: each batch's passages are all 128 or all 512 tokens long; both lengths occur. `query_batch`: the batch among the 4 batches of the query's group.
All inputs are finite; a program needn't handle non-finite values.
Results may differ from a plain program's by a relative error of at most 0.013.
Values sent between devices are 32-bit elements; how exact they have to be, the bound alone decides.
No kernel may reach another device: no remote copies, remote signals or barrier semaphores. Data moves between devices by JAX's collectives and lax.ppermute only.
A program may use at most 192 MiB of HBM per device.

v0:
```python
from functools import partial

import jax
import jax.numpy as jnp
from jax import lax
from jax.sharding import PartitionSpec as P

HEADS = 12
HEAD = 64
LONG = 512
QLEN = 32
BATCH_PB = 4


NEG = -1e30
HIGH = lax.Precision.HIGHEST
LN_EPS = 1e-12


def project(left, right):
    return jnp.dot(left, right, preferred_element_type=jnp.float32)


def project_back(left, right):
    return lax.dot_general(
        left, right, (((1,), (1,)), ((), ())), preferred_element_type=jnp.float32
    )


def contract_rows(left, right):
    return lax.dot_general(
        left, right, (((0,), (0,)), ((), ())), preferred_element_type=jnp.float32
    )


def column_sum(matrix):
    return jnp.sum(matrix, axis=0, dtype=jnp.float32)


def norm_forward(total, gain, shift):
    centred = total - jnp.mean(total, axis=-1, keepdims=True)
    inverse = lax.rsqrt(jnp.mean(centred * centred, axis=-1, keepdims=True) + LN_EPS)
    normed = centred * inverse
    return (normed * gain + shift, normed, inverse)


def norm_backward(grad, normed, inverse, gain):
    scaled = grad * gain
    centred = scaled - jnp.mean(scaled, axis=-1, keepdims=True)
    return inverse * (centred - normed * jnp.mean(scaled * normed, axis=-1, keepdims=True))


def split_heads(matrix):
    return matrix.reshape(matrix.shape[0], HEADS, HEAD)


def attend_forward(query, key, value, segment):
    logits = jnp.einsum(
        "qhd,khd->hqk", split_heads(query), split_heads(key), preferred_element_type=jnp.float32
    ) * HEAD ** (-0.5)
    allowed = (segment[:, None] == segment[None, :])[None]
    logits = jnp.where(allowed, logits, NEG)
    highest = jnp.max(logits, axis=-1, keepdims=True)
    powers = jnp.exp(logits - highest)
    totals = jnp.sum(powers, axis=-1, keepdims=True)
    weights = (powers / totals).astype(jnp.bfloat16)
    mixed = jnp.einsum(
        "hqk,khd->qhd", weights, split_heads(value), preferred_element_type=jnp.float32
    )
    return (mixed.reshape(query.shape[0], -1), highest + jnp.log(totals))


def attend_backward(query, key, value, segment, log_total, grad_mixed):
    scale = HEAD ** (-0.5)
    heads_query = split_heads(query)
    heads_key = split_heads(key)
    heads_value = split_heads(value)
    heads_grad = split_heads(grad_mixed)
    logits = (
        jnp.einsum("qhd,khd->hqk", heads_query, heads_key, preferred_element_type=jnp.float32)
        * scale
    )
    allowed = (segment[:, None] == segment[None, :])[None]
    weights = jnp.where(allowed, jnp.exp(logits - log_total), 0.0)
    grad_weights = jnp.einsum(
        "qhd,khd->hqk", heads_grad, heads_value, preferred_element_type=jnp.float32
    )
    grad_value = jnp.einsum(
        "hqk,qhd->khd", weights.astype(jnp.bfloat16), heads_grad, preferred_element_type=jnp.float32
    )
    grad_logits = (
        weights * (grad_weights - jnp.sum(weights * grad_weights, axis=-1, keepdims=True))
    ).astype(jnp.bfloat16)
    grad_query = (
        jnp.einsum("hqk,khd->qhd", grad_logits, heads_key, preferred_element_type=jnp.float32)
        * scale
    )
    grad_key = (
        jnp.einsum("hqk,qhd->khd", grad_logits, heads_query, preferred_element_type=jnp.float32)
        * scale
    )
    length = query.shape[0]
    return jnp.concatenate(
        [
            grad_query.reshape(length, -1),
            grad_key.reshape(length, -1),
            grad_value.reshape(length, -1),
        ],
        axis=1,
    )


def on_device(
    passages,
    queries,
    passage_ids,
    query_ids,
    batch_length,
    query_batch,
    project_in,
    project_out,
    expand_weight,
    expand_bias,
    reduce_weight,
    norm_gains,
    biases,
    term_weight,
    term_bias,
    out_grad,
    score_grad,
):
    axis_count = lax.axis_size("pa")
    group_index = lax.axis_index("pb")
    member_index = lax.axis_index("pa")
    local_batch = member_index // (axis_count // BATCH_PB)
    length = batch_length[group_index * BATCH_PB + local_batch]
    n_pass = passages.shape[0]
    n_query = queries.shape[0]
    width = passages.shape[1]
    tokens = jnp.concatenate([passages, queries], axis=0)
    segments = []
    first = 0
    segments.append((first, LONG, lax.iota(jnp.int32, LONG) // length))
    segments.append((n_pass, n_query, lax.iota(jnp.int32, n_query) // QLEN))
    zero_bias = jnp.zeros_like(biases[0])
    mixed = (
        project(tokens, project_in) + jnp.concatenate([biases[0], zero_bias, biases[1]])
    ).astype(jnp.bfloat16)
    pieces = []
    log_totals = []
    for first, count, segment in segments:
        rows_here = mixed[first : first + count]
        attended_here, log_here = attend_forward(
            rows_here[:, :width],
            rows_here[:, width : 2 * width],
            rows_here[:, 2 * width :],
            segment,
        )
        pieces.append(attended_here)
        log_totals.append(log_here)
    attended = jnp.concatenate(pieces, axis=0).astype(jnp.bfloat16)
    first_out, normed_one, inverse_one = norm_forward(
        tokens.astype(jnp.float32) + project(attended, project_out) + biases[2],
        norm_gains[0],
        biases[4],
    )
    first_low = first_out.astype(jnp.bfloat16)
    expanded = project(first_low, expand_weight) + expand_bias
    hidden = jax.nn.gelu(expanded, approximate=False).astype(jnp.bfloat16)
    second_out, normed_two, inverse_two = norm_forward(
        first_out + project(hidden, reduce_weight) + biases[3], norm_gains[1], biases[5]
    )
    term_pre = jnp.dot(second_out, term_weight, precision=HIGH) + term_bias[0]
    term = jax.nn.softplus(term_pre)
    passage_out = second_out[:n_pass].astype(jnp.bfloat16)
    query_tags = jnp.broadcast_to(query_batch[:, None], (query_batch.shape[0], QLEN)).reshape(-1)
    gathered = lax.all_gather(
        jnp.stack([term[n_pass:], query_ids.astype(jnp.float32), query_tags.astype(jnp.float32)]),
        "pa",
        axis=1,
        tiled=True,
    )
    group_ids = gathered[1].astype(jnp.int32)
    group_mask = (gathered[2].astype(jnp.int32) == local_batch).astype(jnp.float32)
    weighted = gathered[0] * group_mask
    group_queries = score_grad.shape[0]
    slot_count = score_grad.shape[1]
    slot_table = (lax.iota(jnp.int32, n_pass) // length)[:, None] == lax.iota(
        jnp.int32, slot_count
    )[None, :]
    placed = jnp.where(
        slot_table, term[:n_pass].astype(jnp.bfloat16)[:, None], jnp.zeros((), jnp.bfloat16)
    )
    token_grad = jnp.broadcast_to(
        score_grad[:, None, :], (group_queries, QLEN, slot_count)
    ).reshape(-1, slot_count)
    score_weight = (token_grad * weighted[:, None]).astype(jnp.bfloat16)
    first = 0
    matches = (group_ids[:, None] == passage_ids[None, first : first + LONG]).astype(jnp.bfloat16)
    per_token = project(matches, placed)
    placed_grads = contract_rows(matches, score_weight)
    scores = jnp.sum(
        (weighted[:, None] * per_token).reshape(group_queries, QLEN, slot_count), axis=1
    )
    pass_term_grad = jnp.sum(jnp.where(slot_table, placed_grads, 0.0), axis=1)
    query_term_grad = lax.psum_scatter(
        jnp.sum(token_grad * per_token, axis=1) * group_mask, "pa", scatter_dimension=0, tiled=True
    )
    pre_grad = jnp.concatenate([pass_term_grad, query_term_grad]) * jax.nn.sigmoid(term_pre)
    term_weight_grad = jnp.dot(pre_grad, second_out, precision=HIGH)
    term_bias_grad = jnp.sum(pre_grad)
    second_grad = (
        jnp.concatenate(
            [out_grad.astype(jnp.float32), jnp.zeros((n_query, width), jnp.float32)], axis=0
        )
        + pre_grad[:, None] * term_weight[None, :]
    )
    sum_two_grad = norm_backward(second_grad, normed_two, inverse_two, norm_gains[1])
    reduce_out_grad = sum_two_grad.astype(jnp.bfloat16)
    hidden_grad = project_back(reduce_out_grad, reduce_weight)
    expanded_grad = jax.vjp(partial(jax.nn.gelu, approximate=False), expanded)[1](hidden_grad)[
        0
    ].astype(jnp.bfloat16)
    first_grad = project_back(expanded_grad, expand_weight) + sum_two_grad
    sum_one_grad = norm_backward(first_grad, normed_one, inverse_one, norm_gains[0])
    branch_grad = sum_one_grad.astype(jnp.bfloat16)
    attended_grad = project_back(branch_grad, project_out).astype(jnp.bfloat16)
    mixed_parts = []
    for (first, count, segment), log_here in zip(segments, log_totals):
        rows_here = mixed[first : first + count]
        mixed_parts.append(
            attend_backward(
                rows_here[:, :width],
                rows_here[:, width : 2 * width],
                rows_here[:, 2 * width :],
                segment,
                log_here,
                attended_grad[first : first + count],
            )
        )
    mixed_grad = jnp.concatenate(mixed_parts, axis=0).astype(jnp.bfloat16)
    input_grad = project_back(mixed_grad, project_in) + sum_one_grad
    in_local = contract_rows(tokens, mixed_grad)
    out_local = contract_rows(attended, branch_grad)
    expand_local = contract_rows(first_low, expanded_grad)
    reduce_local = contract_rows(hidden, reduce_out_grad)
    gain_one = jnp.sum(first_grad * normed_one, axis=0)
    gain_two = jnp.sum(second_grad * normed_two, axis=0)
    shift_query = column_sum(mixed_grad[:, :width])
    shift_value = column_sum(mixed_grad[:, 2 * width :])
    shift_branch = column_sum(branch_grad)
    shift_reduce = column_sum(reduce_out_grad)
    shift_first = jnp.sum(first_grad, axis=0)
    shift_second = jnp.sum(second_grad, axis=0)
    expand_shift = column_sum(expanded_grad)
    bias_spread = jnp.broadcast_to(term_bias_grad, (axis_count,))
    summed = (
        lax.psum_scatter(in_local, "pa", scatter_dimension=0, tiled=True),
        lax.psum_scatter(out_local, "pa", scatter_dimension=0, tiled=True),
        lax.psum_scatter(expand_local, "pa", scatter_dimension=0, tiled=True),
        lax.psum_scatter(reduce_local, "pa", scatter_dimension=0, tiled=True),
        lax.psum_scatter(gain_one, "pa", scatter_dimension=0, tiled=True),
        lax.psum_scatter(gain_two, "pa", scatter_dimension=0, tiled=True),
        lax.psum_scatter(shift_query, "pa", scatter_dimension=0, tiled=True),
        lax.psum_scatter(shift_value, "pa", scatter_dimension=0, tiled=True),
        lax.psum_scatter(shift_branch, "pa", scatter_dimension=0, tiled=True),
        lax.psum_scatter(shift_reduce, "pa", scatter_dimension=0, tiled=True),
        lax.psum_scatter(shift_first, "pa", scatter_dimension=0, tiled=True),
        lax.psum_scatter(shift_second, "pa", scatter_dimension=0, tiled=True),
        lax.psum_scatter(expand_shift, "pa", scatter_dimension=0, tiled=True),
        lax.psum_scatter(term_weight_grad, "pa", scatter_dimension=0, tiled=True),
        lax.psum_scatter(bias_spread, "pa", scatter_dimension=0, tiled=True),
    )
    totals = lax.psum(
        (
            summed[0],
            summed[1],
            summed[2],
            summed[3],
            summed[4],
            summed[5],
            summed[6],
            summed[7],
            summed[8],
            summed[9],
            summed[10],
            summed[11],
            summed[12],
            summed[13],
            summed[14],
        ),
        "pb",
    )
    matrices = totals[:4]
    vectors = totals[4:]
    gains_grad = jnp.stack([vectors[0], vectors[1]])
    biases_grad = jnp.stack(
        [vectors[2], vectors[3], vectors[4], vectors[5], vectors[6], vectors[7]]
    )
    return (
        scores,
        passage_out,
        input_grad[:n_pass].astype(jnp.bfloat16),
        input_grad[n_pass:].astype(jnp.bfloat16),
        matrices[0],
        matrices[1],
        matrices[2],
        vectors[8],
        matrices[3],
        gains_grad,
        biases_grad,
        vectors[9],
        vectors[10],
    )


def solution(mesh):
    return jax.shard_map(
        on_device,
        mesh=mesh,
        in_specs=(
            P(("pb", "pa"), None),
            P(("pb", "pa"), None),
            P(("pb", "pa")),
            P(("pb", "pa")),
            P(),
            P(("pb", "pa")),
            P(),
            P(),
            P(),
            P(),
            P(),
            P(),
            P(),
            P(),
            P(),
            P(("pb", "pa"), None),
            P("pb", "pa"),
        ),
        out_specs=(
            P("pb", "pa"),
            P(("pb", "pa"), None),
            P(("pb", "pa"), None),
            P(("pb", "pa"), None),
            P("pa", None),
            P("pa", None),
            P("pa", None),
            P("pa"),
            P("pa", None),
            P(None, "pa"),
            P(None, "pa"),
            P("pa"),
            P(),
        ),
        check_vma=False,
    )
```

profile of v0, /device:TPU:0, one launch (start us, length us, event | category | flops | bytes accessed | tf_op | source)
XLA Modules:
  0.0 810.3 jit_solution(9783464482452830051)
XLA Ops:
  11.9 2.5 add_convert_fusion.1
  22.6 1.7 broadcast_compare_fusion
  24.2 2.3 copy.72
  26.5 1.8 copy.76
  28.3 1.7 copy.75
  30.0 1.7 copy.74
  31.7 2.3 copy.71
  34.0 2.3 copy.70
  38.0 2.0 convolution_convert_fusion.2
  40.1 2.1 select_reduce_fusion
  42.2 3.7 fusion
  46.8 14.9 %fusion.23 = bf16[12,64,512]{2,1,0:T(8,128)(2,1)S(1)} fusion(bf16[512,12,64]{0,2,1:T(8,128)(2,1)} %bitcast.110, f32[12,512,512]{1,2,0:T(8,128)S(1)} %get-tuple-element.80, f32[12,512]{1,0:T(8,128)S(1)} %fusion, f32[12,512]{1,0:T(8,128)S(1)} %get-tuple-element.79, pred[512,512]{0,1:T(8,128)(4,1)} %broadcast_compare_fusion), kind=kOutput, calls=%fused_computation.66 | convolution fusion | flops 418775040 | bytes 14467072 | tf_op jit(solution)/shard_map/hqk,khd->qhd/dot_general | solution.py:67
  63.4 24.3 %multiply_convert_fusion.1 = (bf16[640,3072]{1,0:T(8,128)(2,1)S(1)}, f32[640,3072]{1,0:T(8,128)}, f32[640,3072]{1,0:T(8,128)}) fusion(f32[3072]{0:T(1024)S(1)} %copy-done.72, bf16[768,3072]{1,0:T(8,128)(2,1)} %param.25, f32[640,768]{1,0:T(8,128)S(1)} %get-tuple-element.82, f32[768]{0:T(1024)S(1)} %copy-done.46, f32[768]{0:T(1024)S(1)} %copy-done.40, ...), kind=kOutput, calls=%fused_computation.11 | convolution fusion | flops 3152117760 | bytes 26369024 | tf_op jit(solution)/shard_map/dot_general | solution.py:21
  87.7 3.4 fusion.80
  92.0 1.7 convolution_reduce_fusion.1
  94.5 27.8 %all_gather.3 = f32[3,1024]{1,0:T(4,128)S(1)} all-gather(f32[3,128]{1,0:T(4,128)S(1)} %pad_maximum_fusion.4), channel_id=1, replica_groups=mesh['pb'=4,'pa'=8] {'pa'}, dimensions={1}, use_global_device_ids=true | all-gather | bytes 13824 | tf_op jit(solution)/shard_map/all_gather | solution.py:177
  127.1 1.8 fusion.29
  128.9 1.9 multiply_reduce_fusion.9
  132.1 20.8 %all-reduce.1 = f32[1024]{0:T(1024)} all-reduce(f32[1024]{0:T(1024)} %broadcast_select_fusion), channel_id=2, replica_groups=mesh['pb'=4,'pa'=8] {'pa'}, use_global_device_ids=true, to_apply=%region_11.12.clone | all-reduce | flops 1024 | bytes 8192
  156.9 3.4 multiply_reduce_fusion.1
  160.3 2.9 convert_reduce_fusion.1
  163.3 11.6 %convert_reduce_fusion = (f32[3072]{0:T(1024)}, bf16[640,3072]{1,0:T(8,128)(2,1)S(1)}) fusion(f32[640,3072]{1,0:T(8,128)} %get-tuple-element.66, bf16[3072,768]{1,0:T(8,128)(2,1)} %param.27, f32[640,768]{1,0:T(8,128)S(1)} %get-tuple-element.60, f32[640,3072]{1,0:T(8,128)} %get-tuple-element.83, f32[3072]{0:T(1024)S(1)} %copy-done.73), kind=kOutput, calls=%fused_computation.9 | convolution fusion | flops 3053810688 | bytes 26370048 | tf_op jit(solution)/shard_map/dot_general | solution.py:25
  175.0 4.4 multiply_reduce_fusion.2
  181.9 2.5 fusion.37
  187.2 2.9 convolution_convert_fusion
  191.7 2.3 copy.78
  194.0 1.7 copy.82
  195.8 1.8 multiply_reduce_fusion.8
  199.4 11.8 %multiply_reduce_fusion = (f32[12,512]{1,0:T(8,128)S(1)}, f32[12,512,512]{1,2,0:T(8,128)}) fusion(f32[12,512,512]{1,2,0:T(8,128)} %copy-done.1, f32[12,512]{1,0:T(8,128)S(1)} %copy-done.39, pred[512,512]{0,1:T(8,128)(4,1)S(1)} %copy-done.15, bf16[512,12,64]{0,2,1:T(8,128)(2,1)S(1)} %bitcast.112, bf16[512,12,64]{0,2,1:T(8,128)(2,1)S(1)} %bitcast.111), kind=kOutput, calls=%fused_computation.1 | convolution fusion | flops 418375680 | bytes 27049984 | tf_op jit(solution)/shard_map/qhd,khd->hqk/dot_general | solution.py:85
  212.8 7.1 multiply_convert_fusion
  220.0 2.0 multiply_convert_fusion.2
  223.2 2.6 fusion.20
  226.7 7.9 fusion.68
  235.3 10.6 %fusion.69 = f32[768,3072]{1,0:T(8,128)} fusion(bf16[640,3072]{1,0:T(8,128)(2,1)} %copy-done.17, f32[640,768]{1,0:T(8,128)} %copy-done.7, f32[768]{0:T(1024)S(1)} %copy-done.47, f32[768]{0:T(1024)S(1)} %copy-done.42, f32[640]{0:T(1024)S(1)} %copy-done.45, f32[640]{0:T(1024)S(1)} %copy-done.37), kind=kOutput, calls=%fused_computation.171 | convolution fusion | flops 3022356480 | bytes 15346688 | tf_op jit(solution)/shard_map/dot_general | solution.py:31
  246.0 10.3 %fusion.55 = f32[3072,768]{1,0:T(8,128)} fusion(bf16[640,3072]{1,0:T(8,128)(2,1)} %copy-done.77, f32[640,768]{1,0:T(8,128)} %copy-done.21), kind=kOutput, calls=%fused_computation.159 | convolution fusion | flops 3020390400 | bytes 15335424 | tf_op jit(solution)/shard_map/dot_general | solution.py:31
  256.6 126.2 %reduce-scatter.5.cloned.1.call-done = f32[96,2304]{1,0:T(8,128)} async-done(((f32[768,2304]{1,0:T(8,128)}), f32[96,2304]{1,0:T(8,128)}) %reduce-scatter.5.cloned.1.call-update) | async-done | bytes 884752 | tf_op jit(solution)/shard_map/reduce_scatter | solution.py:258
  382.8 166.6 %reduce-scatter.9.cloned.1.call-done = f32[96,3072]{1,0:T(8,128)} async-done(((f32[768,3072]{1,0:T(8,128)}), f32[96,3072]{1,0:T(8,128)}) %reduce-scatter.9.cloned.1.call-update) | async-done | bytes 1179664 | tf_op jit(solution)/shard_map/reduce_scatter | solution.py:260
  549.4 166.5 %reduce-scatter.11.cloned.1.call-done = f32[384,768]{1,0:T(8,128)} async-done(((f32[3072,768]{1,0:T(8,128)}), f32[384,768]{1,0:T(8,128)}) %reduce-scatter.11.cloned.1.call-update) | async-done | bytes 1179664 | tf_op jit(solution)/shard_map/reduce_scatter | solution.py:261
  715.9 5.1 add_convert_fusion.2
  721.6 2.4 slice.154
  729.8 2.6 convolution_reduce_fusion
  732.4 3.7 convert_reduce_fusion.3
  737.3 36.8 %all-reduce.13 = (f32[3072]{0:T(1024)}, f32[768]{0:T(1024)}, f32[768]{0:T(1024)}, f32[768]{0:T(1024)}, f32[768]{0:T(1024)}, /*index=5*/f32[768]{0:T(1024)}, f32[...) all-reduce(f32[3072]{0:T(1024)} %get-tuple-element.91, ...), channel_id=6, replica_groups=mesh['pb'=4,'pa'=8] {'pa'}, use_global_device_ids=true, to_apply=%region_25.26.clone | all-reduce | flops 9992 | bytes 79936
  774.1 1.9 dynamic-slice.23
  786.7 7.0 all-reduce.14
  796.2 2.2 copy.100
  798.4 1.7 copy.101
  800.1 2.4 copy.102
  (257 shorter events, 60.3 us)
Async XLA Ops:
  7.2 4.7 copy-start
  7.2 249.4 %reduce-scatter.7.cloned.1.call-start = ((), (), s32[]{:S(2)}) async-start(), calls=%async_computation.5 | async-start | bytes 2654208 | tf_op jit(solution)/shard_map/reduce_scatter | solution.py:259
  14.4 4.7 copy-start.76
  14.4 6.7 copy-start.58
  42.2 4.6 copy-start.1
  46.0 15.7 %copy-start.51 = (f32[12,512]{1,0:T(8,128)}, f32[12,512]{1,0:T(8,128)S(1)}, u32[]{:S(2)}) copy-start(f32[12,512]{1,0:T(8,128)S(1)} %fusion) | copy-start | bytes 73732
  46.8 14.9 %copy-start.33 = (bf16[640,768]{1,0:T(8,128)(2,1)S(1)}, bf16[640,768]{1,0:T(8,128)(2,1)}, u32[]{:S(2)}) copy-start(bf16[640,768]{1,0:T(8,128)(2,1)} %copy-done.32) | copy-start | bytes 2949124
  46.8 14.9 %copy-start.48 = (bf16[12,64,128]{2,1,0:T(8,128)(2,1)S(1)}, bf16[12,64,128]{2,1,0:T(8,128)(2,1)}, u32[]{:S(2)}) copy-start(bf16[12,64,128]{2,1,0:T(8,128)(2,1)} %convolution_convert_fusion.2) | copy-start | bytes 589828
  46.8 14.9 %copy-start.67 = (f32[768]{0:T(1024)S(1)}, f32[768]{0:T(1024)}, u32[]{:S(2)}) copy-start(f32[768]{0:T(1024)} %get-tuple-element.25) | copy-start | bytes 9220
  46.8 14.9 %copy-start.71 = (bf16[768,768]{1,0:T(8,128)(2,1)S(1)}, bf16[768,768]{1,0:T(8,128)(2,1)}, u32[]{:S(2)}) copy-start(bf16[768,768]{1,0:T(8,128)(2,1)} %param.24) | copy-start | bytes 3538948
  61.8 25.9 %slice-start.3 = ((s8[4718592]{0:T(1024)(128)(4,1)}), s8[4194304]{0:T(1024)(128)(4,1)S(1)}, s32[]{:S(2)}) async-start(s8[4718592]{0:T(1024)(128)(4,1)} %bitcast.144), calls=%async_computation.12 | async-start | bytes 8388608
  62.9 24.8 %copy-start.7 = (f32[640,768]{1,0:T(8,128)}, f32[640,768]{1,0:T(8,128)S(1)}, u32[]{:S(2)}) copy-start(f32[640,768]{1,0:T(8,128)S(1)} %get-tuple-element.82) | copy-start | bytes 5898244
  62.9 24.7 %copy-start.35 = (f32[640]{0:T(1024)}, f32[640]{0:T(1024)S(1)}, u32[]{:S(2)}) copy-start(f32[640]{0:T(1024)S(1)} %broadcast_multiply_fusion.6) | copy-start | bytes 7684
  63.3 24.4 %copy-start.43 = (f32[640]{0:T(1024)}, f32[640]{0:T(1024)S(1)}, u32[]{:S(2)}) copy-start(f32[640]{0:T(1024)S(1)} %add_rsqrt_fusion.1) | copy-start | bytes 7684
  63.4 24.3 %copy-start.66 = (f32[768]{0:T(1024)S(1)}, f32[768]{0:T(1024)}, u32[]{:S(2)}) copy-start(f32[768]{0:T(1024)} %get-tuple-element.28) | copy-start | bytes 9220
  63.4 24.3 %slice-start.4 = ((s8[4718592]{0:T(1024)(128)(4,1)}), s8[524288]{0:T(1024)(128)(4,1)S(1)}, s32[]{:S(2)}) async-start(s8[4718592]{0:T(1024)(128)(4,1)} %bitcast.144), calls=%async_computation.13 | async-start | bytes 1048576
  91.2 32.2 %copy-start.68 = (f32[32,4]{0,1:T(4,128)S(1)}, f32[32,4]{0,1:T(4,128)}, u32[]{:S(2)}) copy-start(f32[32,4]{0,1:T(4,128)} %param.33) | copy-start | bytes 1540
  93.8 29.6 %copy-start.59 = (f32[640]{0:T(1024)}, f32[640]{0:T(1024)S(1)}, u32[]{:S(2)}) copy-start(f32[640]{0:T(1024)S(1)} %convolution_reduce_fusion.1) | copy-start | bytes 7684
  154.7 5.6 copy-start.3
  154.7 8.5 %copy-start.73 = (f32[3072]{0:T(1024)S(1)}, f32[3072]{0:T(1024)}, u32[]{:S(2)}) copy-start(f32[3072]{0:T(1024)} %param.26) | copy-start | bytes 36868
  156.9 6.3 copy-start.54
  160.3 14.6 %slice-start.5 = ((s8[4718592]{0:T(1024)(128)(4,1)}), s8[4194304]{0:T(1024)(128)(4,1)S(1)}, s32[]{:S(2)}) async-start(s8[4718592]{0:T(1024)(128)(4,1)} %bitcast.146), calls=%async_computation.14 | async-start | bytes 8388608
  163.2 11.7 %copy-start.21 = (f32[640,768]{1,0:T(8,128)}, f32[640,768]{1,0:T(8,128)S(1)}, u32[]{:S(2)}) copy-start(f32[640,768]{1,0:T(8,128)S(1)} %get-tuple-element.60) | copy-start | bytes 5898244
  163.2 11.7 %copy-start.8 = (f32[640,768]{1,0:T(8,128)S(1)}, f32[640,768]{1,0:T(8,128)}, u32[]{:S(2)}) copy-start(f32[640,768]{1,0:T(8,128)} %copy-done.7) | copy-start | bytes 5898244
  163.2 11.7 %copy-start.36 = (f32[640]{0:T(1024)S(1)}, f32[640]{0:T(1024)}, u32[]{:S(2)}) copy-start(f32[640]{0:T(1024)} %copy-done.35) | copy-start | bytes 7684
  163.3 11.7 %copy-start.41 = (f32[768]{0:T(1024)S(1)}, f32[768]{0:T(1024)}, u32[]{:S(2)}) copy-start(f32[768]{0:T(1024)} %get-tuple-element.93) | copy-start | bytes 9220
  163.3 11.7 %copy-start.44 = (f32[640]{0:T(1024)S(1)}, f32[640]{0:T(1024)}, u32[]{:S(2)}) copy-start(f32[640]{0:T(1024)} %copy-done.43) | copy-start | bytes 7684
  163.3 11.7 %slice-start.6 = ((s8[4718592]{0:T(1024)(128)(4,1)}), s8[524288]{0:T(1024)(128)(4,1)S(1)}, s32[]{:S(2)}) async-start(s8[4718592]{0:T(1024)(128)(4,1)} %bitcast.146), calls=%async_computation.15 | async-start | bytes 1048576
  184.4 198.4 %reduce-scatter.5.cloned.1.call-start = ((), (), s32[]{:S(2)}) async-start(), calls=%async_computation.4 | async-start | bytes 7962624 | tf_op jit(solution)/shard_map/reduce_scatter | solution.py:258
  199.3 26.5 %copy-start.27 = (bf16[12,64,128]{2,1,0:T(8,128)(2,1)}, bf16[12,64,128]{2,1,0:T(8,128)(2,1)S(1)}, u32[]{:S(2)}) copy-start(bf16[12,64,128]{2,1,0:T(8,128)(2,1)S(1)} %fusion.25) | copy-start | bytes 589828
  199.3 12.6 %slice-start = ((s8[12582912]{0:T(1024)(128)(4,1)}), s8[4194304]{0:T(1024)(128)(4,1)S(1)}, s32[]{:S(2)}) async-start(s8[12582912]{0:T(1024)(128)(4,1)} %bitcast.101), calls=%async_computation.9 | async-start | bytes 8388608
  199.4 11.8 %copy-start.22 = (bf16[128,768]{0,1:T(8,128)(2,1)S(1)}, bf16[128,768]{0,1:T(8,128)(2,1)}, u32[]{:S(2)}) copy-start(bf16[128,768]{0,1:T(8,128)(2,1)} %copy.76) | copy-start | bytes 589828
  199.4 12.1 %copy-start.6 = (f32[12,128,128]{1,2,0:T(8,128)S(1)}, f32[12,128,128]{1,2,0:T(8,128)}, u32[]{:S(2)}) copy-start(f32[12,128,128]{1,2,0:T(8,128)} %copy-done.5) | copy-start | bytes 2359300
  199.4 12.1 %copy-start.24 = (bf16[128,768]{0,1:T(8,128)(2,1)S(1)}, bf16[128,768]{0,1:T(8,128)(2,1)}, u32[]{:S(2)}) copy-start(bf16[128,768]{0,1:T(8,128)(2,1)} %copy.82) | copy-start | bytes 589828
  199.4 12.1 %copy-start.50 = (f32[12,128]{1,0:T(8,128)S(1)}, f32[12,128]{1,0:T(8,128)}, u32[]{:S(2)}) copy-start(f32[12,128]{1,0:T(8,128)} %log_add_fusion.1) | copy-start | bytes 18436
  199.4 12.5 %slice-start.1 = ((s8[12582912]{0:T(1024)(128)(4,1)}), s8[4194304]{0:T(1024)(128)(4,1)S(1)}, s32[]{:S(2)}) async-start(s8[12582912]{0:T(1024)(128)(4,1)} %bitcast.101), calls=%async_computation.10 | async-start | bytes 8388608
  199.4 13.4 %slice-start.2 = ((s8[12582912]{0:T(1024)(128)(4,1)}), s8[4194304]{0:T(1024)(128)(4,1)S(1)}, s32[]{:S(2)}) async-start(s8[12582912]{0:T(1024)(128)(4,1)} %bitcast.101), calls=%async_computation.11 | async-start | bytes 8388608
  211.5 14.4 %copy-start.28 = (bf16[12,64,128]{2,1,0:T(8,128)(2,1)}, bf16[12,64,128]{2,1,0:T(8,128)(2,1)S(1)}, u32[]{:S(2)}) copy-start(bf16[12,64,128]{2,1,0:T(8,128)(2,1)S(1)} %fusion.24) | copy-start | bytes 589828
  211.9 14.0 %copy-start.26 = (bf16[12,64,128]{2,1,0:T(8,128)(2,1)}, bf16[12,64,128]{2,1,0:T(8,128)(2,1)S(1)}, u32[]{:S(2)}) copy-start(bf16[12,64,128]{2,1,0:T(8,128)(2,1)S(1)} %convolution_convert_fusion.1) | copy-start | bytes 589828
  212.8 7.2 copy-start.13
  234.6 314.8 %reduce-scatter.9.cloned.1.call-start = ((), (), s32[]{:S(2)}) async-start(), calls=%async_computation.6 | async-start | bytes 10616832 | tf_op jit(solution)/shard_map/reduce_scatter | solution.py:260
  245.9 469.9 %reduce-scatter.11.cloned.1.call-start = ((), (), s32[]{:S(2)}) async-start(), calls=%async_computation.7 | async-start | bytes 10616832 | tf_op jit(solution)/shard_map/reduce_scatter | solution.py:261
  256.3 539.9 %all-reduce.18.cloned.1.call-start = ((), (), s32[]{:S(2)}) async-start(), calls=%async_computation.8 | async-start | bytes 7077888 | tf_op jit(solution)/shard_map/psum | solution.py:274
  715.9 5.1 copy-start.55
  723.9 13.4 %copy-start.61 = (f32[768]{0:T(1024)S(1)}, f32[768]{0:T(1024)}, u32[]{:S(2)}) copy-start(f32[768]{0:T(1024)} %get-tuple-element.17) | copy-start | bytes 9220
  723.9 13.4 %copy-start.62 = (f32[768]{0:T(1024)S(1)}, f32[768]{0:T(1024)}, u32[]{:S(2)}) copy-start(f32[768]{0:T(1024)} %get-tuple-element.22) | copy-start | bytes 9220
  723.9 13.4 %copy-start.63 = (f32[768]{0:T(1024)S(1)}, f32[768]{0:T(1024)}, u32[]{:S(2)}) copy-start(f32[768]{0:T(1024)} %get-tuple-element.59) | copy-start | bytes 9220
  796.2 6.3 copy-start.25
  (42 other events, 110.5 us)
Sparse Core Ops, SparseCore 0:
  184.5 66.4 reduce-scatter.6
  254.7 128.0 reduce-scatter.4
  386.8 162.4 reduce-scatter.8
  553.2 162.5 reduce-scatter.10
  718.5 74.6 all-reduce.17
where the time goes:
time: 814 us; the launch traced here: 810 us
  waiting for transfers between devices  459 us (56%)
  matrix products  135 us (17%)
  blocking collectives  92.4 us (11%)
  local copies, waits for them, and re-layouts  64.1 us (8%)
  other arithmetic  40.1 us (5%)
  between operations  18.4 us (2%)
    reduce_scatter x1, waiting for transfers between devices, on_device(): lax.psum_scatter(expand_local, 'pa', scatter_dimension=0, tiled=True)  167 us
    reduce_scatter x1, waiting for transfers between devices, on_device(): lax.psum_scatter(reduce_local, 'pa', scatter_dimension=0, tiled=True)  166 us
    reduce_scatter x1, waiting for transfers between devices, on_device(): lax.psum_scatter(in_local, 'pa', scatter_dimension=0, tiled=True)  126 us
    unnamed x2, blocking collectives  57.6 us
    dot_general x5, matrix products, project(): return jnp.dot(left, right, preferred_element_type=jnp.float32)  33.2 us
    dot_general x5, matrix products, contract_rows(): lax.dot_general(left, right, (((0,), (0,)), ((), ())), preferred_element_...  33.1 us
    all_gather x1, blocking collectives, on_device(): lax.all_gather(jnp.stack([term[n_pass:], query_ids.astype(jnp.float32), q...  27.8 us
    dot_general x4, matrix products, project_back(): lax.dot_general(left, right, (((1,), (1,)), ((), ())), preferred_element_...  23.9 us
  transfers between devices with their start and end apart: 5, of which 3 were waited for; matrix products, arithmetic and copies ran while one was open for 13% of the time, Pallas kernels for 0%

commit v1 on v0

--- a/solution.py
+++ b/solution.py
@@ -108,6 +108,124 @@
         ],
         axis=1,
     )
+
+
+GROUP_FIRST = (("pb", 2), ("pa", 1))
+ROW_FIRST = (("pa", 1), ("pb", 2))
+
+
+def swap(value, axis, distance):
+    return lax.ppermute(
+        value, axis, [(i, i ^ distance) for i in range(lax.axis_size(axis))]
+    )
+
+
+def bit(axis, distance):
+    return (lax.axis_index(axis) // distance) % 2
+
+
+def pick(value, index, dim):
+    return lax.dynamic_index_in_dim(value, index, dim, keepdims=False)
+
+
+def group_gather(mine):
+    count = lax.axis_size("pa")
+    me = lax.axis_index("pa")
+    ahead = [mine]
+    for shift in range(1, count):
+        ahead.append(
+            lax.ppermute(mine, "pa", [((i + shift) % count, i) for i in range(count)])
+        )
+    twice = jnp.concatenate(ahead + ahead, axis=1)
+    width = mine.shape[1]
+    return lax.dynamic_slice_in_dim(twice, (count - me) * width, count * width, axis=1)
+
+
+def group_scatter(whole):
+    count = lax.axis_size("pa")
+    me = lax.axis_index("pa")
+    blocks = whole.reshape(count, -1)
+    total = pick(blocks, me, 0)
+    for shift in range(1, count):
+        block = pick(blocks, (me + shift) % count, 0)
+        total = total + lax.ppermute(
+            block, "pa", [(i, (i + shift) % count) for i in range(count)]
+        )
+    return total
+
+
+def steps_of(order):
+    steps = [(axis, distance) for axis, distance in order]
+    distance = 2
+    while distance < lax.axis_size("pa"):
+        steps.append(("pa", distance))
+        distance *= 2
+    return steps
+
+
+def tree_sum(send, keep, order):
+    names = []
+    distance = lax.axis_size("pa") // 2
+    while distance:
+        names.append(("pa", distance))
+        distance //= 2
+    names.append(("pb", 2))
+    received = swap(send, "pb", 1)
+    for axis, distance in steps_of(order):
+        dim = names.index((axis, distance))
+        names.pop(dim)
+        mine = bit(axis, distance)
+        send = pick(keep, 1 - mine, dim) + pick(received, 1 - mine, dim)
+        keep = pick(keep, mine, dim) + pick(received, mine, dim)
+        received = swap(send, axis, distance)
+    mine = keep + received
+    other = swap(mine, "pb", 2)
+    high = bit("pb", 2)
+    return jnp.where(high == 0, jnp.stack([mine, other]), jnp.stack([other, mine]))
+
+
+def cut(matrix):
+    bits = lax.axis_size("pa").bit_length() - 1
+    rows = matrix.shape[0] >> (bits + 1)
+    return matrix.reshape((2,) * (bits + 1) + (rows, matrix.shape[1]))
+
+
+def summed_rows(left, right, order):
+    core = bit("pb", 1)
+    half = right.shape[1] // 2
+    parts = [
+        cut(contract_rows(left, lax.dynamic_slice_in_dim(right, side * half, half, axis=1)))
+        for side in (1 - core, core)
+    ]
+    mine = tree_sum(parts[0], parts[1], order)
+    mine = mine.reshape(-1, half)
+    other = swap(mine, "pb", 1)
+    return jnp.where(
+        core == 0, jnp.concatenate([mine, other], 1), jnp.concatenate([other, mine], 1)
+    )
+
+
+def summed_vectors(vectors):
+    count = lax.axis_size("pa")
+    core = bit("pb", 1)
+    shares = [v.reshape(count, -1) for v in vectors]
+    packed = jnp.concatenate(shares, axis=1)
+    used = packed.shape[1]
+    lanes = -(-used // 512) * 128
+    packed = jnp.pad(packed, ((0, 0), (0, 4 * lanes - used)))
+    packed = packed.reshape(count, 2, 2, 1, lanes)
+    parts = [pick(packed, 1 - core, 2), pick(packed, core, 2)]
+    parts = [p.reshape((2,) * (count.bit_length() - 1) + (2, 1, lanes)) for p in parts]
+    mine = tree_sum(parts[0], parts[1], GROUP_FIRST)
+    other = swap(mine, "pb", 1)
+    both = jnp.where(core == 0, jnp.stack([mine, other], 1), jnp.stack([other, mine], 1))
+    flat = both.reshape(-1)
+    totals = []
+    first = 0
+    for share in shares:
+        totals.append(flat[first : first + share.shape[1]])
+        first += share.shape[1]
+    return totals
 
 
 def on_device(
@@ -174,11 +292,8 @@
     term = jax.nn.softplus(term_pre)
     passage_out = second_out[:n_pass].astype(jnp.bfloat16)
     query_tags = jnp.broadcast_to(query_batch[:, None], (query_batch.shape[0], QLEN)).reshape(-1)
-    gathered = lax.all_gather(
-        jnp.stack([term[n_pass:], query_ids.astype(jnp.float32), query_tags.astype(jnp.float32)]),
-        "pa",
-        axis=1,
-        tiled=True,
+    gathered = group_gather(
+        jnp.stack([term[n_pass:], query_ids.astype(jnp.float32), query_tags.astype(jnp.float32)])
     )
     group_ids = gathered[1].astype(jnp.int32)
     group_mask = (gathered[2].astype(jnp.int32) == local_batch).astype(jnp.float32)
@@ -203,9 +318,7 @@
         (weighted[:, None] * per_token).reshape(group_queries, QLEN, slot_count), axis=1
     )
     pass_term_grad = jnp.sum(jnp.where(slot_table, placed_grads, 0.0), axis=1)
-    query_term_grad = lax.psum_scatter(
-        jnp.sum(token_grad * per_token, axis=1) * group_mask, "pa", scatter_dimension=0, tiled=True
-    )
+    query_term_grad = group_scatter(jnp.sum(token_grad * per_token, axis=1) * group_mask)
     pre_grad = jnp.concatenate([pass_term_grad, query_term_grad]) * jax.nn.sigmoid(term_pre)
     term_weight_grad = jnp.dot(pre_grad, second_out, precision=HIGH)
     term_bias_grad = jnp.sum(pre_grad)
@@ -240,10 +353,10 @@
         )
     mixed_grad = jnp.concatenate(mixed_parts, axis=0).astype(jnp.bfloat16)
     input_grad = project_back(mixed_grad, project_in) + sum_one_grad
-    in_local = contract_rows(tokens, mixed_grad)
-    out_local = contract_rows(attended, branch_grad)
-    expand_local = contract_rows(first_low, expanded_grad)
-    reduce_local = contract_rows(hidden, reduce_out_grad)
+    reduce_total = summed_rows(hidden, reduce_out_grad, ROW_FIRST)
+    expand_total = summed_rows(first_low, expanded_grad, GROUP_FIRST)
+    out_total = summed_rows(attended, branch_grad, GROUP_FIRST)
+    in_total = summed_rows(tokens, mixed_grad, ROW_FIRST)
     gain_one = jnp.sum(first_grad * normed_one, axis=0)
     gain_two = jnp.sum(second_grad * normed_two, axis=0)
     shift_query = column_sum(mixed_grad[:, :width])
@@ -253,46 +366,22 @@
     shift_first = jnp.sum(first_grad, axis=0)
     shift_second = jnp.sum(second_grad, axis=0)
     expand_shift = column_sum(expanded_grad)
-    bias_spread = jnp.broadcast_to(term_bias_grad, (axis_count,))
-    summed = (
-        lax.psum_scatter(in_local, "pa", scatter_dimension=0, tiled=True),
-        lax.psum_scatter(out_local, "pa", scatter_dimension=0, tiled=True),
-        lax.psum_scatter(expand_local, "pa", scatter_dimension=0, tiled=True),
-        lax.psum_scatter(reduce_local, "pa", scatter_dimension=0, tiled=True),
-        lax.psum_scatter(gain_one, "pa", scatter_dimension=0, tiled=True),
-        lax.psum_scatter(gain_two, "pa", scatter_dimension=0, tiled=True),
-        lax.psum_scatter(shift_query, "pa", scatter_dimension=0, tiled=True),
-        lax.psum_scatter(shift_value, "pa", scatter_dimension=0, tiled=True),
-        lax.psum_scatter(shift_branch, "pa", scatter_dimension=0, tiled=True),
-        lax.psum_scatter(shift_reduce, "pa", scatter_dimension=0, tiled=True),
-        lax.psum_scatter(shift_first, "pa", scatter_dimension=0, tiled=True),
-        lax.psum_scatter(shift_second, "pa", scatter_dimension=0, tiled=True),
-        lax.psum_scatter(expand_shift, "pa", scatter_dimension=0, tiled=True),
-        lax.psum_scatter(term_weight_grad, "pa", scatter_dimension=0, tiled=True),
-        lax.psum_scatter(bias_spread, "pa", scatter_dimension=0, tiled=True),
-    )
-    totals = lax.psum(
-        (
-            summed[0],
-            summed[1],
-            summed[2],
-            summed[3],
-            summed[4],
-            summed[5],
-            summed[6],
-            summed[7],
-            summed[8],
-            summed[9],
-            summed[10],
-            summed[11],
-            summed[12],
-            summed[13],
-            summed[14],
-        ),
-        "pb",
-    )
-    matrices = totals[:4]
-    vectors = totals[4:]
+    vectors = summed_vectors(
+        [
+            gain_one,
+            gain_two,
+            shift_query,
+            shift_value,
+            shift_branch,
+            shift_reduce,
+            shift_first,
+            shift_second,
+            expand_shift,
+            term_weight_grad,
+            jnp.broadcast_to(term_bias_grad, (axis_count,)),
+        ]
+    )
+    matrices = (in_total, out_total, expand_total, reduce_total)
     gains_grad = jnp.stack([vectors[0], vectors[1]])
     biases_grad = jnp.stack(
         [vectors[2], vectors[3], vectors[4], vectors[5], vectors[6], vectors[7]]

time: 814 us -> 493 us (0.61)
  waiting for transfers between devices: 459 us -> 140 us
  blocking collectives: 92.4 us -> 0 us
  starting transfers between devices: 0.59 us -> 52.7 us
  other arithmetic: 40.1 us -> 87.6 us
  between operations: 18.4 us -> 3.99 us
  matrix products: 135 us -> 125 us
  local copies, waits for them, and re-layouts: 64.1 us -> 73.6 us
    reduce_scatter x4 -> x0, waiting for transfers between devices: 459 us -> none  [the longest x1 167 us: on_device(): lax.psum_scatter(expand_local, 'pa', scatter_dimension=0, tiled=True)]
    ppermute x0 -> x49, waiting for transfers between devices: none -> 140 us  [the longest x35 136 us: swap(): lax.ppermute(value, axis, [(i, i ^ distance) for i in range(lax.axis_size...]
    unnamed x2 -> x0, blocking collectives: 57.6 us -> none
    ppermute x0 -> x49, starting transfers between devices: none -> 52.7 us  [the longest x35 29.6 us: swap(): lax.ppermute(value, axis, [(i, i ^ distance) for i in range(lax.axis_size...]
    add x0 -> x26, other arithmetic: none -> 40 us  [the longest x14 35 us: tree_sum(): keep = pick(keep, mine, dim) + pick(received, mine, dim)]
    all_gather x1 -> x0, blocking collectives: 27.8 us -> none  [on_device(): lax.all_gather(jnp.stack([term[n_pass:], query_ids.astype(jnp.float32), q...]
    reshape x0 -> x13, local copies, waits for them, and re-layouts: none -> 12.8 us  [the longest x11 10.1 us: summed_vectors(): shares = [v.reshape(count, -1) for v in vectors]]
    dot_general x2, matrix products: 16.9 us -> 7.15 us  [attend_forward(): jnp.einsum('hqk,khd->qhd', weights, split_heads(value), preferred_element...]
  transfers between devices with their start and end apart: 5 -> 49, of which waited for: 3 -> 15; matrix products, arithmetic and copies ran while one was open for 13% -> 26% of each run, Pallas kernels for 0% -> 0%
where the time goes in v1:
time: 493 us; the launch traced here: 484 us
  waiting for transfers between devices  140 us (28%)
  matrix products  125 us (25%)
  other arithmetic  87.6 us (18%)
  local copies, waits for them, and re-layouts  73.6 us (15%)
  starting transfers between devices  52.7 us (11%)
    ppermute x35, waiting for transfers between devices, swap(): lax.ppermute(value, axis, [(i, i ^ distance) for i in range(lax.axis_size...  136 us
    add x14, other arithmetic, tree_sum(): keep = pick(keep, mine, dim) + pick(received, mine, dim)  35 us
    dot_general x5, matrix products, project(): return jnp.dot(left, right, preferred_element_type=jnp.float32)  33.5 us
    ppermute x35, starting transfers between devices, swap(): lax.ppermute(value, axis, [(i, i ^ distance) for i in range(lax.axis_size...  29.6 us
    dot_general x9, matrix products, contract_rows(): lax.dot_general(left, right, (((0,), (0,)), ((), ())), preferred_element_...  29 us
    unnamed x259, local copies, waits for them, and re-layouts  20.9 us
    dot_general x4, matrix products, project_back(): lax.dot_general(left, right, (((1,), (1,)), ((), ())), preferred_element_...  19.5 us
    dot_general x2, matrix products, attend_backward(): jnp.einsum('qhd,khd->hqk', heads_grad, heads_value, preferred_element_typ...  14.8 us
  transfers between devices with their start and end apart: 49, of which 15 were waited for; matrix products, arithmetic and copies ran while one was open for 26% of the time, Pallas kernels for 0%

profile of v1, /device:TPU:0, one launch (start us, length us, event | category | flops | bytes accessed | tf_op | source)
XLA Modules:
  0.0 483.6 jit_solution(16420967013650236795)
XLA Ops:
  5.3 2.5 add_convert_fusion.1
  35.6 3.7 fusion
  40.4 5.1 %fusion.31 = bf16[12,64,512]{2,1,0:T(8,128)(2,1)S(1)} fusion(bf16[512,12,64]{0,2,1:T(8,128)(2,1)} %bitcast.338, f32[12,512,512]{1,2,0:T(8,128)S(1)} %get-tuple-element.107, f32[12,512]{1,0:T(8,128)S(1)} %fusion, f32[12,512]{1,0:T(8,128)S(1)} %get-tuple-element.106, pred[512,512]{0,1:T(8,128)(4,1)} %broadcast_compare_fusion), kind=kOutput, calls=%fused_computation.80 | convolution fusion | flops 418775040 | bytes 14467072 | tf_op jit(solution)/shard_map/hqk,khd->qhd/dot_general | solution.py:67
  47.2 24.6 %multiply_convert_fusion.1 = (bf16[640,3072]{1,0:T(8,128)(2,1)S(1)}, f32[640,3072]{1,0:T(8,128)}, f32[640,3072]{1,0:T(8,128)}) fusion(f32[3072]{0:T(1024)S(1)} %copy-done.103, bf16[768,3072]{1,0:T(8,128)(2,1)} %param.25, f32[640,768]{1,0:T(8,128)S(1)} %get-tuple-element.109, f32[768]{0:T(1024)S(1)} %copy-done.89, f32[768]{0:T(1024)S(1)} %copy-done.77, ...), kind=kOutput, calls=%fused_computation.11 | convolution fusion | flops 3152117760 | bytes 26369024 | tf_op jit(solution)/shard_map/dot_general | solution.py:21
  71.9 3.4 fusion.137
  80.2 3.0 collective-permute-start.5
  83.2 2.5 collective-permute-start.4
  87.0 2.6 collective-permute-start.2
  124.5 2.6 collective-permute-start.13
  128.2 3.0 collective-permute-start.10
  133.9 2.8 collective-permute-done.9
  139.1 3.5 multiply_reduce_fusion.1
  144.5 11.3 %convert_reduce_fusion = (f32[3072]{0:T(1024)}, bf16[640,3072]{1,0:T(8,128)(2,1)S(1)}) fusion(f32[640,3072]{1,0:T(8,128)} %get-tuple-element.43, f32[640,3072]{1,0:T(8,128)} %get-tuple-element.110, f32[3072]{0:T(1024)S(1)} %copy-done.104, bf16[640,768]{1,0:T(8,128)(2,1)S(1)} %get-tuple-element.36, bf16[3072,768]{1,0:T(8,128)(2,1)} %param.27), kind=kOutput, calls=%fused_computation.9 | convolution fusion | flops 3053319168 | bytes 25387008 | tf_op jit(solution)/shard_map/dot_general | solution.py:25
  155.9 4.7 multiply_reduce_fusion.2
  160.6 2.5 convert_reduce_fusion.2
  170.7 3.1 multiply_reduce_fusion.8
  176.2 7.4 %fusion.28 = bf16[12,64,512]{2,1,0:T(8,128)(2,1)S(1)} fusion(bf16[512,12,64]{0,2,1:T(8,128)(2,1)} %bitcast.340, f32[12,512,512]{1,2,0:T(8,128)} %copy-done.1, f32[12,512]{1,0:T(8,128)} %log_add_fusion, pred[512,512]{0,1:T(8,128)(4,1)} %broadcast_compare_fusion), kind=kOutput, calls=%fused_computation.79 | convolution fusion | flops 415629312 | bytes 14442496 | tf_op jit(solution)/shard_map/hqk,qhd->khd/dot_general | solution.py:88
  183.8 11.7 %multiply_reduce_fusion = (f32[12,512]{1,0:T(8,128)S(1)}, f32[12,512,512]{1,2,0:T(8,128)}) fusion(f32[12,512,512]{1,2,0:T(8,128)} %copy-done.1, f32[12,512]{1,0:T(8,128)S(1)} %copy-done.51, pred[512,512]{0,1:T(8,128)(4,1)S(1)} %copy-done.20, bf16[512,12,64]{0,2,1:T(8,128)(2,1)S(1)} %bitcast.341, bf16[512,12,64]{0,2,1:T(8,128)(2,1)S(1)} %bitcast.339), kind=kOutput, calls=%fused_computation.1 | convolution fusion | flops 418375680 | bytes 27049984 | tf_op jit(solution)/shard_map/qhd,khd->hqk/dot_general | solution.py:85
  196.1 6.3 %fusion.16 = f32[768,1536]{1,0:T(8,128)} fusion(bf16[640,3072]{1,0:T(8,128)(2,1)} %copy-done.113, s32[]{:T(128)S(6)} %select_n.549, f32[640,768]{1,0:T(8,128)S(1)} %copy-done.14, f32[768]{0:T(1024)S(1)} %copy-done.90, f32[768]{0:T(1024)S(1)} %copy-done.79, f32[640]{0:T(1024)S(1)} %copy-done.84, f32[640]{0:T(1024)S(1)} %copy-done.68), kind=kOutput, calls=%fused_computation.45 | convolution fusion | flops 1512407040 | bytes 8662020 | tf_op jit(solution)/shard_map/dot_general | solution.py:31
  202.4 7.1 %multiply_convert_fusion = bf16[12,512,512]{1,2,0:T(8,128)(2,1)S(1)} fusion(f32[12,512,512]{1,2,0:T(8,128)} %get-tuple-element.117, f32[12,512,512]{1,2,0:T(8,128)S(1)} %bitcast.328, f32[12,512]{1,0:T(8,128)S(1)} %get-tuple-element.116, f32[12,512]{1,0:T(8,128)S(1)} %copy-done.51, pred[512,512]{0,1:T(8,128)(4,1)S(1)} %copy-done.20), kind=kLoop, calls=%fused_computation | loop fusion | flops 18874368 | bytes 31768576 | tf_op jit(solution)/shard_map/convert_element_type | solution.py:93
  213.1 7.4 %maximum_maximum_fusion = bf16[640,2304]{0,1:T(8,128)(2,1)S(1)} fusion(bf16[128,768]{0,1:T(8,128)(2,1)S(1)} %bitcast.360, bf16[128,768]{0,1:T(8,128)(2,1)S(1)} %bitcast.362, bf16[128,768]{0,1:T(8,128)(2,1)S(1)} %bitcast.364, bf16[512,768]{0,1:T(8,128)(2,1)S(1)} %bitcast.366, bf16[512,768]{0,1:T(8,128)(2,1)S(1)} %bitcast.342, bf16[512,768]{0,1:T(8,128)(2,1)S(1)} %bitcast.333), kind=kLoop, calls=%fused_computation.30 | loop fusion | flops 17694720 | bytes 5898240 | tf_op jit(solution)/shard_map/concatenate | solution.py:354
  220.5 3.5 fusion.24
  225.3 4.4 fusion.51
  230.2 2.6 convolution_reduce_fusion
  240.2 3.2 fusion.55
  249.3 3.5 fusion.26
  255.2 5.5 %dynamic-slice_add_fusion.1 = (f32[2,2,2,1,48,1536]{5,4,3,2,1,0:T(8,128)}, f32[2,2,2,48,1536]{4,3,2,1,0:T(8,128)}) fusion(f32[2,2,2,2,48,1536]{5,4,3,2,1,0:T(8,128)} %collective-permute-done.28, s32[]{:T(128)S(6)} %select_n.526, f32[2,2,2,2,48,1536]{5,4,3,2,1,0:T(8,128)S(1)} %bitcast.336, s32[]{:T(128)S(6)} %select_n.530), kind=kLoop, calls=%fused_computation.38 | loop fusion | flops 1179648 | bytes 14155784 | tf_op jit(solution)/shard_map/add | solution.py:179
  262.2 4.3 dynamic-slice_add_fusion.2
  273.4 41.4 %collective-permute-done.36 = f32[2,2,2,1,384]{4,2,1,0,3:T(2,128)} collective-permute-done((f32[2,2,2,1,384]{4,2,1,0,3:T(2,128)}, f32[2,2,2,1,384]{4,2,1,0,3:T(2,128)}, u32[]{:S(2)}, u32[]{:S(2)}) %collective-permute-start.36) | collective-permute-done | bytes 12320 | tf_op jit(solution)/shard_map/ppermute | solution.py:118
  319.5 2.4 dynamic-slice_add_fusion.3
  323.4 2.5 fusion.53
  326.5 2.4 collective-permute-start.39
  328.9 5.4 %dynamic-slice_add_fusion = (f32[2,2,1,2,192,384]{5,4,3,2,1,0:T(8,128)}, f32[2,2,2,192,384]{4,3,2,1,0:T(8,128)}) fusion(f32[2,2,2,2,192,384]{5,4,3,2,1,0:T(8,128)} %collective-permute-done.42, s32[]{:T(128)S(6)} %select_n.524, f32[2,2,2,2,192,384]{5,4,3,2,1,0:T(8,128)S(1)} %bitcast.335, s32[]{:T(128)S(6)} %select_n.527), kind=kLoop, calls=%fused_computation.36 | loop fusion | flops 1179648 | bytes 14155784 | tf_op jit(solution)/shard_map/add | solution.py:179
  334.8 2.4 slice.214
  344.5 2.9 bitcast_add_fusion.5
  349.0 3.6 bitcast_add_fusion.3
  353.3 2.5 add_convert_fusion.2
  358.7 36.5 %collective-permute-done.23 = f32[2,2,48,384]{3,2,1,0:T(8,128)} collective-permute-done((f32[2,2,48,384]{3,2,1,0:T(8,128)}, f32[2,2,48,384]{3,2,1,0:T(8,128)}, u32[]{:S(2)}, u32[]{:S(2)}) %collective-permute-start.23) | collective-permute-done | bytes 294944 | tf_op jit(solution)/shard_map/ppermute | solution.py:118
  400.3 2.7 bitcast_add_fusion.1
  404.5 2.4 collective-permute-start.25
  408.3 8.6 %collective-permute-done.30 = f32[2,2,48,1536]{3,2,1,0:T(8,128)} collective-permute-done((f32[2,2,48,1536]{3,2,1,0:T(8,128)}, f32[2,2,48,1536]{3,2,1,0:T(8,128)}, u32[]{:S(2)}, u32[]{:S(2)}) %collective-permute-start.30) | collective-permute-done | bytes 1179680 | tf_op jit(solution)/shard_map/ppermute | solution.py:118
  421.7 5.7 %collective-permute-done.26 = f32[48,384]{1,0:T(8,128)S(1)} collective-permute-done((f32[48,384]{1,0:T(8,128)S(1)}, f32[48,384]{1,0:T(8,128)S(1)}, u32[]{:S(2)}, u32[]{:S(2)}) %collective-permute-start.26) | collective-permute-done | bytes 73760 | tf_op jit(solution)/shard_map/ppermute | solution.py:118
  427.5 2.4 collective-permute-start.18
  430.8 4.1 collective-permute-start.32
  434.9 6.3 %collective-permute-done.18 = f32[48,1152]{1,0:T(8,128)S(1)} collective-permute-done((f32[48,1152]{1,0:T(8,128)S(1)}, f32[48,1152]{1,0:T(8,128)S(1)}, u32[]{:S(2)}, u32[]{:S(2)}) %collective-permute-start.18) | collective-permute-done | bytes 221216 | tf_op jit(solution)/shard_map/ppermute | solution.py:118
  441.9 14.0 %collective-permute-done.45 = f32[2,192,384]{2,1,0:T(8,128)S(1)} collective-permute-done((f32[2,192,384]{2,1,0:T(8,128)S(1)}, f32[2,192,384]{2,1,0:T(8,128)S(1)}, u32[]{:S(2)}, u32[]{:S(2)}) %collective-permute-start.45) | collective-permute-done | bytes 589856 | tf_op jit(solution)/shard_map/ppermute | solution.py:118
  456.9 14.0 %collective-permute-done.46 = f32[192,384]{1,0:T(8,128)S(1)} collective-permute-done((f32[192,384]{1,0:T(8,128)S(1)}, f32[192,384]{1,0:T(8,128)S(1)}, u32[]{:S(2)}, u32[]{:S(2)}) %collective-permute-start.46) | collective-permute-done | bytes 294944 | tf_op jit(solution)/shard_map/ppermute | solution.py:118
  472.4 7.5 %collective-permute-done.47 = f32[192,384]{1,0:T(8,128)S(1)} collective-permute-done((f32[192,384]{1,0:T(8,128)S(1)}, f32[192,384]{1,0:T(8,128)S(1)}, u32[]{:S(2)}, u32[]{:S(2)}) %collective-permute-start.47) | collective-permute-done | bytes 294944 | tf_op jit(solution)/shard_map/ppermute | solution.py:118
  (469 shorter events, 161.8 us)
Async XLA Ops:
  80.2 26.5 %collective-permute-start.5 = (f32[3,128]{1,0:T(4,128)}, f32[3,128]{1,0:T(4,128)}, u32[]{:S(2)}, u32[]{:S(2)}) collective-permute-start(f32[3,128]{1,0:T(4,128)} %get-tuple-element.102), channel_id=1, source_target_pairs={{6,0},{7,1},{0,2},{1,3},{2,4},{3,5},{4,6},{5,7},{14,8},{15,9},{8,1... | collective-permute-start | bytes 4616 | tf_op jit(solution)/shard_map/ppermute | solution.py:137
  83.2 22.2 %collective-permute-start.4 = (f32[3,128]{1,0:T(4,128)}, f32[3,128]{1,0:T(4,128)}, u32[]{:S(2)}, u32[]{:S(2)}) collective-permute-start(f32[3,128]{1,0:T(4,128)} %get-tuple-element.102), channel_id=1, source_target_pairs={{5,0},{6,1},{7,2},{0,3},{1,4},{2,5},{3,6},{4,7},{13,8},{14,9},{15,... | collective-permute-start | bytes 4616 | tf_op jit(solution)/shard_map/ppermute | solution.py:137
  85.8 18.4 %collective-permute-start.3 = (f32[3,128]{1,0:T(4,128)}, f32[3,128]{1,0:T(4,128)}, u32[]{:S(2)}, u32[]{:S(2)}) collective-permute-start(f32[3,128]{1,0:T(4,128)} %get-tuple-element.102), channel_id=1, source_target_pairs={{4,0},{5,1},{6,2},{7,3},{0,4},{1,5},{2,6},{3,7},{12,8},{13,9},{14,... | collective-permute-start | bytes 4616 | tf_op jit(solution)/shard_map/ppermute | solution.py:137
  87.0 15.9 %collective-permute-start.2 = (f32[3,128]{1,0:T(4,128)}, f32[3,128]{1,0:T(4,128)}, u32[]{:S(2)}, u32[]{:S(2)}) collective-permute-start(f32[3,128]{1,0:T(4,128)} %get-tuple-element.102), channel_id=1, source_target_pairs={{3,0},{4,1},{5,2},{6,3},{7,4},{0,5},{1,6},{2,7},{11,8},{12,9},{13,... | collective-permute-start | bytes 4616 | tf_op jit(solution)/shard_map/ppermute | solution.py:137
  89.7 8.3 %collective-permute-start = (f32[3,128]{1,0:T(4,128)}, f32[3,128]{1,0:T(4,128)}, u32[]{:S(2)}, u32[]{:S(2)}) collective-permute-start(f32[3,128]{1,0:T(4,128)} %get-tuple-element.102), channel_id=1, source_target_pairs={{1,0},{2,1},{3,2},{4,3},{5,4},{6,5},{7,6},{0,7},{9,8},{10,9},{11,1... | collective-permute-start | bytes 4616 | tf_op jit(solution)/shard_map/ppermute | solution.py:137
  98.0 3.8 collective-permute-start.1
  101.7 6.5 %collective-permute-start.6 = (f32[3,128]{1,0:T(4,128)}, f32[3,128]{1,0:T(4,128)S(1)}, u32[]{:S(2)}, u32[]{:S(2)}) collective-permute-start(f32[3,128]{1,0:T(4,128)} %get-tuple-element.102), channel_id=1, source_target_pairs={{7,0},{0,1},{1,2},{2,3},{3,4},{4,5},{5,6},{6,7},{15,8},{8,9},{9,10... | collective-permute-start | bytes 4616 | tf_op jit(solution)/shard_map/ppermute | solution.py:137
  122.3 8.9 %collective-permute-start.7 = (f32[128]{0:T(128)}, f32[128]{0:T(128)}, u32[]{:S(2)}, u32[]{:S(2)}) collective-permute-start(f32[128]{0:T(128)} %get-tuple-element.95), channel_id=1, source_target_pairs={{0,1},{1,2},{2,3},{3,4},{4,5},{5,6},{6,7},{7,0},{8,9},{9,10},{10,1... | collective-permute-start | bytes 1544 | tf_op jit(solution)/shard_map/ppermute | solution.py:151
  124.5 6.7 %collective-permute-start.13 = (f32[128]{0:T(128)}, f32[128]{0:T(128)}, u32[]{:S(2)}, u32[]{:S(2)}) collective-permute-start(f32[128]{0:T(128)} %get-tuple-element.96), channel_id=1, source_target_pairs={{0,7},{1,0},{2,1},{3,2},{4,3},{5,4},{6,5},{7,6},{8,15},{9,8},{10,9... | collective-permute-start | bytes 1544 | tf_op jit(solution)/shard_map/ppermute | solution.py:151
  127.1 6.8 %collective-permute-start.12 = (f32[128]{0:T(128)}, f32[128]{0:T(128)S(1)}, u32[]{:S(2)}, u32[]{:S(2)}) collective-permute-start(f32[128]{0:T(128)} %get-tuple-element.97), channel_id=1, source_target_pairs={{0,6},{1,7},{2,0},{3,1},{4,2},{5,3},{6,4},{7,5},{8,14},{9,15},{10,... | collective-permute-start | bytes 1544 | tf_op jit(solution)/shard_map/ppermute | solution.py:151
  128.2 5.7 %collective-permute-start.11 = (f32[128]{0:T(128)}, f32[128]{0:T(128)S(1)}, u32[]{:S(2)}, u32[]{:S(2)}) collective-permute-start(f32[128]{0:T(128)} %get-tuple-element.98), channel_id=1, source_target_pairs={{0,5},{1,6},{2,7},{3,0},{4,1},{5,2},{6,3},{7,4},{8,13},{9,14},{10,... | collective-permute-start | bytes 1544 | tf_op jit(solution)/shard_map/ppermute | solution.py:151
  128.2 5.7 %collective-permute-start.10 = (f32[128]{0:T(128)}, f32[128]{0:T(128)S(1)}, u32[]{:S(2)}, u32[]{:S(2)}) collective-permute-start(f32[128]{0:T(128)} %get-tuple-element.99), channel_id=1, source_target_pairs={{0,4},{1,5},{2,6},{3,7},{4,0},{5,1},{6,2},{7,3},{8,12},{9,13},{10,... | collective-permute-start | bytes 1544 | tf_op jit(solution)/shard_map/ppermute | solution.py:151
  131.2 5.5 %collective-permute-start.9 = (f32[128]{0:T(128)}, f32[128]{0:T(128)S(1)}, u32[]{:S(2)}, u32[]{:S(2)}) collective-permute-start(f32[128]{0:T(128)} %get-tuple-element.100), channel_id=1, source_target_pairs={{0,3},{1,4},{2,5},{3,6},{4,7},{5,0},{6,1},{7,2},{8,11},{9,12},{10,... | collective-permute-start | bytes 1544 | tf_op jit(solution)/shard_map/ppermute | solution.py:151
  131.2 5.9 %collective-permute-start.8 = (f32[128]{0:T(128)}, f32[128]{0:T(128)S(1)}, u32[]{:S(2)}, u32[]{:S(2)}) collective-permute-start(f32[128]{0:T(128)} %get-tuple-element.101), channel_id=1, source_target_pairs={{0,2},{1,3},{2,4},{3,5},{4,6},{5,7},{6,0},{7,1},{8,10},{9,11},{10,... | collective-permute-start | bytes 1544 | tf_op jit(solution)/shard_map/ppermute | solution.py:151
  202.4 52.8 %collective-permute-start.28 = (f32[2,2,2,2,48,1536]{5,4,3,2,1,0:T(8,128)}, f32[2,2,2,2,48,1536]{5,4,3,2,1,0:T(8,128)}, u32[]{:S(2)}, u32[]{:S(2)}) collective-permute-start(f32[2,2,2,2,48,1536]{5,4,3,2,1,0:T(8,128)} %bitcast.72), channel_id=1, source_target_pairs={{0,8},{8,0},{16,24},{24,16},{1,9},{9,1},{17,25},{25,17},{2,10},{10... | collective-permute-start | bytes 14155784 | tf_op jit(solution)/shard_map/ppermute | solution.py:118
  224.1 38.2 %collective-permute-start.14 = (f32[2,2,2,2,48,1152]{5,4,3,2,1,0:T(8,128)}, f32[2,2,2,2,48,1152]{5,4,3,2,1,0:T(8,128)}, u32[]{:S(2)}, u32[]{:S(2)}) collective-permute-start(f32[2,2,2,2,48,1152]{5,4,3,2,1,0:T(8,128)} %bitcast.40), channel_id=1, source_target_pairs={{0,8},{8,0},{16,24},{24,16},{1,9},{9,1},{17,25},{25,17},{2,10},{10... | collective-permute-start | bytes 10616840 | tf_op jit(solution)/shard_map/ppermute | solution.py:118
  229.6 99.3 %collective-permute-start.42 = (f32[2,2,2,2,192,384]{5,4,3,2,1,0:T(8,128)}, f32[2,2,2,2,192,384]{5,4,3,2,1,0:T(8,128)}, u32[]{:S(2)}, u32[]{:S(2)}) collective-permute-start(f32[2,2,2,2,192,384]{5,4,3,2,1,0:T(8,128)} %bitcast.105), channel_id=1, source_target_pairs={{0,8},{8,0},{16,24},{24,16},{1,9},{9,1},{17,25},{25,17},{2,10},{10... | collective-permute-start | bytes 14155784 | tf_op jit(solution)/shard_map/ppermute | solution.py:118
  243.4 76.1 %collective-permute-start.21 = (f32[2,2,2,2,48,384]{5,4,3,2,1,0:T(8,128)}, f32[2,2,2,2,48,384]{5,4,3,2,1,0:T(8,128)}, u32[]{:S(2)}, u32[]{:S(2)}) collective-permute-start(f32[2,2,2,2,48,384]{5,4,3,2,1,0:T(8,128)} %bitcast.56), channel_id=1, source_target_pairs={{0,8},{8,0},{16,24},{24,16},{1,9},{9,1},{17,25},{25,17},{2,10},{10... | collective-permute-start | bytes 3538952 | tf_op jit(solution)/shard_map/ppermute | solution.py:118
  260.7 88.2 %collective-permute-start.29 = (f32[2,2,2,48,1536]{4,3,2,1,0:T(8,128)}, f32[2,2,2,48,1536]{4,3,2,1,0:T(8,128)}, u32[]{:S(2)}, u32[]{:S(2)}) collective-permute-start(f32[2,2,2,48,1536]{4,3,2,1,0:T(8,128)} %get-tuple-element.47), channel_id=1, source_target_pairs={{0,16},{8,24},{16,0},{24,8},{1,17},{9,25},{17,1},{25,9},{2,18},{10... | collective-permute-start | bytes 7077896 | tf_op jit(solution)/shard_map/ppermute | solution.py:118
  266.5 78.0 %collective-permute-start.15 = (f32[2,2,2,48,1152]{4,3,2,1,0:T(8,128)}, f32[2,2,2,48,1152]{4,3,2,1,0:T(8,128)}, u32[]{:S(2)}, u32[]{:S(2)}) collective-permute-start(f32[2,2,2,48,1152]{4,3,2,1,0:T(8,128)} %get-tuple-element.49), channel_id=1, source_target_pairs={{0,1},{1,0},{2,3},{3,2},{4,5},{5,4},{6,7},{7,6},{8,9},{9,8},{10,11... | collective-permute-start | bytes 5308424 | tf_op jit(solution)/shard_map/ppermute | solution.py:118
  270.0 1.5 collective-permute-start.35
  272.9 41.9 %collective-permute-start.36 = (f32[2,2,2,1,384]{4,2,1,0,3:T(2,128)}, f32[2,2,2,1,384]{4,2,1,0,3:T(2,128)}, u32[]{:S(2)}, u32[]{:S(2)}) collective-permute-start(f32[2,2,2,1,384]{4,2,1,0,3:T(2,128)} %get-tuple-element.75), channel_id=1, source_target_pairs={{0,16},{8,24},{16,0},{24,8},{1,17},{9,25},{17,1},{25,9},{2,18},{10... | collective-permute-start | bytes 36872 | tf_op jit(solution)/shard_map/ppermute | solution.py:118
  315.7 3.7 collective-permute-start.37
  319.4 6.5 %collective-permute-start.38 = (f32[2,1,384]{2,1,0:T(1,128)S(1)}, f32[2,1,384]{2,1,0:T(1,128)S(1)}, u32[]{:S(2)}, u32[]{:S(2)}) collective-permute-start(f32[2,1,384]{2,1,0:T(1,128)S(1)} %get-tuple-element.85), channel_id=1, source_target_pairs={{0,2},{1,3},{2,0},{3,1},{4,6},{5,7},{6,4},{7,5},{8,10},{9,11},{10,... | collective-permute-start | bytes 9224 | tf_op jit(solution)/shard_map/ppermute | solution.py:118
  321.9 18.9 %collective-permute-start.22 = (f32[2,2,2,48,384]{4,3,2,1,0:T(8,128)}, f32[2,2,2,48,384]{4,3,2,1,0:T(8,128)}, u32[]{:S(2)}, u32[]{:S(2)}) collective-permute-start(f32[2,2,2,48,384]{4,3,2,1,0:T(8,128)} %get-tuple-element.67), channel_id=1, source_target_pairs={{0,16},{8,24},{16,0},{24,8},{1,17},{9,25},{17,1},{25,9},{2,18},{10... | collective-permute-start | bytes 1769480 | tf_op jit(solution)/shard_map/ppermute | solution.py:118
  326.5 12.9 %collective-permute-start.39 = (f32[1,384]{1,0:T(1,128)}, f32[1,384]{1,0:T(1,128)}, u32[]{:S(2)}, u32[]{:S(2)}) collective-permute-start(f32[1,384]{1,0:T(1,128)} %fusion.105), channel_id=1, source_target_pairs={{0,4},{1,5},{2,6},{3,7},{4,0},{5,1},{6,2},{7,3},{8,12},{9,13},{10,... | collective-permute-start | bytes 4616 | tf_op jit(solution)/shard_map/ppermute | solution.py:118
  334.3 66.0 %collective-permute-start.43 = (f32[2,2,2,192,384]{4,3,2,1,0:T(8,128)}, f32[2,2,2,192,384]{4,3,2,1,0:T(8,128)}, u32[]{:S(2)}, u32[]{:S(2)}) collective-permute-start(f32[2,2,2,192,384]{4,3,2,1,0:T(8,128)} %get-tuple-element.45), channel_id=1, source_target_pairs={{0,1},{1,0},{2,3},{3,2},{4,5},{5,4},{6,7},{7,6},{8,9},{9,8},{10,11... | collective-permute-start | bytes 7077896 | tf_op jit(solution)/shard_map/ppermute | solution.py:118
  340.2 17.1 %collective-permute-start.40 = (f32[1,384]{1,0:T(1,128)S(1)}, f32[1,384]{1,0:T(1,128)S(1)}, u32[]{:S(2)}, u32[]{:S(2)}) collective-permute-start(f32[1,384]{1,0:T(1,128)S(1)} %fusion.103), channel_id=1, source_target_pairs={{0,16},{8,24},{16,0},{24,8},{1,17},{9,25},{17,1},{25,9},{2,18},{10... | collective-permute-start | bytes 4616 | tf_op jit(solution)/shard_map/ppermute | solution.py:118
  342.9 52.2 %collective-permute-start.23 = (f32[2,2,48,384]{3,2,1,0:T(8,128)}, f32[2,2,48,384]{3,2,1,0:T(8,128)}, u32[]{:S(2)}, u32[]{:S(2)}) collective-permute-start(f32[2,2,48,384]{3,2,1,0:T(8,128)} %get-tuple-element.71), channel_id=1, source_target_pairs={{0,1},{1,0},{2,3},{3,2},{4,5},{5,4},{6,7},{7,6},{8,9},{9,8},{10,11... | collective-permute-start | bytes 884744 | tf_op jit(solution)/shard_map/ppermute | solution.py:118
  347.4 59.5 %collective-permute-start.16 = (f32[2,2,48,1152]{3,2,1,0:T(8,128)}, f32[2,2,48,1152]{3,2,1,0:T(8,128)}, u32[]{:S(2)}, u32[]{:S(2)}) collective-permute-start(f32[2,2,48,1152]{3,2,1,0:T(8,128)} %get-tuple-element.55), channel_id=1, source_target_pairs={{0,16},{8,24},{16,0},{24,8},{1,17},{9,25},{17,1},{25,9},{2,18},{10... | collective-permute-start | bytes 2654216 | tf_op jit(solution)/shard_map/ppermute | solution.py:118
  352.5 64.5 %collective-permute-start.30 = (f32[2,2,48,1536]{3,2,1,0:T(8,128)}, f32[2,2,48,1536]{3,2,1,0:T(8,128)}, u32[]{:S(2)}, u32[]{:S(2)}) collective-permute-start(f32[2,2,48,1536]{3,2,1,0:T(8,128)} %get-tuple-element.53), channel_id=1, source_target_pairs={{0,1},{1,0},{2,3},{3,2},{4,5},{5,4},{6,7},{7,6},{8,9},{9,8},{10,11... | collective-permute-start | bytes 3538952 | tf_op jit(solution)/shard_map/ppermute | solution.py:118
  397.1 6.6 %collective-permute-start.24 = (f32[2,48,384]{2,1,0:T(8,128)}, f32[2,48,384]{2,1,0:T(8,128)}, u32[]{:S(2)}, u32[]{:S(2)}) collective-permute-start(f32[2,48,384]{2,1,0:T(8,128)} %get-tuple-element.73), channel_id=1, source_target_pairs={{0,2},{1,3},{2,0},{3,1},{4,6},{5,7},{6,4},{7,5},{8,10},{9,11},{10,... | collective-permute-start | bytes 442376 | tf_op jit(solution)/shard_map/ppermute | solution.py:118
  403.0 26.9 %collective-permute-start.44 = (f32[2,2,192,384]{3,2,1,0:T(8,128)S(1)}, f32[2,2,192,384]{3,2,1,0:T(8,128)S(1)}, u32[]{:S(2)}, u32[]{:S(2)}) collective-permute-start(f32[2,2,192,384]{3,2,1,0:T(8,128)S(1)} %get-tuple-element.51), channel_id=1, source_target_pairs={{0,16},{8,24},{16,0},{24,8},{1,17},{9,25},{17,1},{25,9},{2,18},{10... | collective-permute-start | bytes 3538952 | tf_op jit(solution)/shard_map/ppermute | solution.py:118
  404.5 15.1 %collective-permute-start.25 = (f32[48,384]{1,0:T(8,128)S(1)}, f32[48,384]{1,0:T(8,128)S(1)}, u32[]{:S(2)}, u32[]{:S(2)}) collective-permute-start(f32[48,384]{1,0:T(8,128)S(1)} %fusion.70), channel_id=1, source_target_pairs={{0,4},{1,5},{2,6},{3,7},{4,0},{5,1},{6,2},{7,3},{8,12},{9,13},{10,... | collective-permute-start | bytes 221192 | tf_op jit(solution)/shard_map/ppermute | solution.py:118
  408.2 19.2 %collective-permute-start.17 = (f32[2,48,1152]{2,1,0:T(8,128)S(1)}, f32[2,48,1152]{2,1,0:T(8,128)S(1)}, u32[]{:S(2)}, u32[]{:S(2)}) collective-permute-start(f32[2,48,1152]{2,1,0:T(8,128)S(1)} %get-tuple-element.69), channel_id=1, source_target_pairs={{0,2},{1,3},{2,0},{3,1},{4,6},{5,7},{6,4},{7,5},{8,10},{9,11},{10,... | collective-permute-start | bytes 1327112 | tf_op jit(solution)/shard_map/ppermute | solution.py:118
  418.4 12.3 %collective-permute-start.31 = (f32[2,48,1536]{2,1,0:T(8,128)S(1)}, f32[2,48,1536]{2,1,0:T(8,128)S(1)}, u32[]{:S(2)}, u32[]{:S(2)}) collective-permute-start(f32[2,48,1536]{2,1,0:T(8,128)S(1)} %get-tuple-element.65), channel_id=1, source_target_pairs={{0,2},{1,3},{2,0},{3,1},{4,6},{5,7},{6,4},{7,5},{8,10},{9,11},{10,... | collective-permute-start | bytes 1769480 | tf_op jit(solution)/shard_map/ppermute | solution.py:118
  420.5 6.8 %collective-permute-start.26 = (f32[48,384]{1,0:T(8,128)S(1)}, f32[48,384]{1,0:T(8,128)S(1)}, u32[]{:S(2)}, u32[]{:S(2)}) collective-permute-start(f32[48,384]{1,0:T(8,128)S(1)} %bitcast_add_fusion.26), channel_id=1, source_target_pairs={{0,16},{8,24},{16,0},{24,8},{1,17},{9,25},{17,1},{25,9},{2,18},{10... | collective-permute-start | bytes 221192 | tf_op jit(solution)/shard_map/ppermute | solution.py:118
  427.4 44.3 %collective-permute-start.27 = (f32[96,384]{1,0:T(8,128)S(1)}, f32[96,384]{1,0:T(8,128)S(1)}, u32[]{:S(2)}, u32[]{:S(2)}) collective-permute-start(f32[96,384]{1,0:T(8,128)S(1)} %bitcast.370), channel_id=1, source_target_pairs={{0,8},{8,0},{16,24},{24,16},{1,9},{9,1},{17,25},{25,17},{2,10},{10... | collective-permute-start | bytes 442376 | tf_op jit(solution)/shard_map/ppermute | solution.py:118
  427.5 13.8 %collective-permute-start.18 = (f32[48,1152]{1,0:T(8,128)S(1)}, f32[48,1152]{1,0:T(8,128)S(1)}, u32[]{:S(2)}, u32[]{:S(2)}) collective-permute-start(f32[48,1152]{1,0:T(8,128)S(1)} %fusion.68), channel_id=1, source_target_pairs={{0,4},{1,5},{2,6},{3,7},{4,0},{5,1},{6,2},{7,3},{8,12},{9,13},{10,... | collective-permute-start | bytes 663560 | tf_op jit(solution)/shard_map/ppermute | solution.py:118
  430.1 25.9 %collective-permute-start.45 = (f32[2,192,384]{2,1,0:T(8,128)S(1)}, f32[2,192,384]{2,1,0:T(8,128)S(1)}, u32[]{:S(2)}, u32[]{:S(2)}) collective-permute-start(f32[2,192,384]{2,1,0:T(8,128)S(1)} %get-tuple-element.63), channel_id=1, source_target_pairs={{0,2},{1,3},{2,0},{3,1},{4,6},{5,7},{6,4},{7,5},{8,10},{9,11},{10,... | collective-permute-start | bytes 1769480 | tf_op jit(solution)/shard_map/ppermute | solution.py:118
  430.8 25.3 %collective-permute-start.32 = (f32[48,1536]{1,0:T(8,128)S(1)}, f32[48,1536]{1,0:T(8,128)S(1)}, u32[]{:S(2)}, u32[]{:S(2)}) collective-permute-start(f32[48,1536]{1,0:T(8,128)S(1)} %fusion.66), channel_id=1, source_target_pairs={{0,4},{1,5},{2,6},{3,7},{4,0},{5,1},{6,2},{7,3},{8,12},{9,13},{10,... | collective-permute-start | bytes 884744 | tf_op jit(solution)/shard_map/ppermute | solution.py:118
  441.3 15.5 %collective-permute-start.19 = (f32[48,1152]{1,0:T(8,128)S(1)}, f32[48,1152]{1,0:T(8,128)S(1)}, u32[]{:S(2)}, u32[]{:S(2)}) collective-permute-start(f32[48,1152]{1,0:T(8,128)S(1)} %bitcast_add_fusion.21), channel_id=1, source_target_pairs={{0,16},{8,24},{16,0},{24,8},{1,17},{9,25},{17,1},{25,9},{2,18},{10... | collective-permute-start | bytes 663560 | tf_op jit(solution)/shard_map/ppermute | solution.py:118
  456.0 14.9 %collective-permute-start.46 = (f32[192,384]{1,0:T(8,128)S(1)}, f32[192,384]{1,0:T(8,128)S(1)}, u32[]{:S(2)}, u32[]{:S(2)}) collective-permute-start(f32[192,384]{1,0:T(8,128)S(1)} %fusion.65), channel_id=1, source_target_pairs={{0,4},{1,5},{2,6},{3,7},{4,0},{5,1},{6,2},{7,3},{8,12},{9,13},{10,... | collective-permute-start | bytes 884744 | tf_op jit(solution)/shard_map/ppermute | solution.py:118
  456.1 15.4 %collective-permute-start.33 = (f32[48,1536]{1,0:T(8,128)S(1)}, f32[48,1536]{1,0:T(8,128)S(1)}, u32[]{:S(2)}, u32[]{:S(2)}) collective-permute-start(f32[48,1536]{1,0:T(8,128)S(1)} %bitcast_add_fusion.16), channel_id=1, source_target_pairs={{0,16},{8,24},{16,0},{24,8},{1,17},{9,25},{17,1},{25,9},{2,18},{10... | collective-permute-start | bytes 884744 | tf_op jit(solution)/shard_map/ppermute | solution.py:118
  456.8 23.3 %collective-permute-start.20 = (f32[96,1152]{1,0:T(8,128)S(1)}, f32[96,1152]{1,0:T(8,128)S(1)}, u32[]{:S(2)}, u32[]{:S(2)}) collective-permute-start(f32[96,1152]{1,0:T(8,128)S(1)} %bitcast.352), channel_id=1, source_target_pairs={{0,8},{8,0},{16,24},{24,16},{1,9},{9,1},{17,25},{25,17},{2,10},{10... | collective-permute-start | bytes 1327112 | tf_op jit(solution)/shard_map/ppermute | solution.py:118
  470.9 9.0 %collective-permute-start.47 = (f32[192,384]{1,0:T(8,128)S(1)}, f32[192,384]{1,0:T(8,128)S(1)}, u32[]{:S(2)}, u32[]{:S(2)}) collective-permute-start(f32[192,384]{1,0:T(8,128)S(1)} %bitcast_add_fusion.13), channel_id=1, source_target_pairs={{0,16},{8,24},{16,0},{24,8},{1,17},{9,25},{17,1},{25,9},{2,18},{10... | collective-permute-start | bytes 884744 | tf_op jit(solution)/shard_map/ppermute | solution.py:118
  471.6 9.4 %collective-permute-start.34 = (f32[96,1536]{1,0:T(8,128)S(1)}, f32[96,1536]{1,0:T(8,128)S(1)}, u32[]{:S(2)}, u32[]{:S(2)}) collective-permute-start(f32[96,1536]{1,0:T(8,128)S(1)} %bitcast.344), channel_id=1, source_target_pairs={{0,8},{8,0},{16,24},{24,16},{1,9},{9,1},{17,25},{25,17},{2,10},{10... | collective-permute-start | bytes 1769480 | tf_op jit(solution)/shard_map/ppermute | solution.py:118
  480.0 2.2 collective-permute-start.48
  (123 other events, 956.6 us)
